TPU v7x, 32 devices: a whole 2x2x4 slice. The times are simulated.
32 devices in a mesh: pole: 4 (over x, core), slab: 8 (over z, y).
Axes of the slice: x: 2, y: 2, z: 4, core: 2. Of those that a mesh axis runs over, the one named last changes fastest.
Arguments:
- vectors: float32 [2, 16, 32, 16, 128], P(None, None, 'slab'), may hold values from -6 to 6
- potential: float32 [32, 16, 128], P('slab'), may hold values from 0 to 2
Outputs:
- filtered: float32 [2, 16, 32, 16, 128], P(None, None, 'slab', 'pole')
- gram_correlation: float32 [2, 16, 16], replicated
- gram_energy: float32 [2, 16, 16], replicated
All inputs are finite; a program needn't handle non-finite values.
Results may differ from a plain program's by a relative error of at most 0.005.
Values sent between devices are 32-bit elements; how exact they have to be, the bound alone decides.
A program may use at most 64 MiB of HBM per device.

v0:
```python
import functools
import math

import jax
import jax.numpy as jnp
from jax import lax
from jax.experimental import pallas as pl
from jax.experimental.pallas import tpu as pltpu
from jax.sharding import PartitionSpec as P

ITERS = 3
CENTER = 2.0
RADIUS = 1.5
BASE = 4.0

MESH = pl.DeviceIdType.MESH


def cmul(a, b):
    return (a[0] * b[0] - a[1] * b[1], a[0] * b[1] + a[1] * b[0])


def cmul_conj(a, b):
    return (a[0] * b[0] + a[1] * b[1], a[0] * b[1] - a[1] * b[0])


def cadd(a, b):
    return (a[0] + b[0], a[1] + b[1])


def csub(a, b):
    return (a[0] - b[0], a[1] - b[1])


def cdiv(n, d):
    inv = 1.0 / (d[0] * d[0] + d[1] * d[1])
    return ((n[0] * d[0] + n[1] * d[1]) * inv, (n[1] * d[0] - n[0] * d[1]) * inv)


def cocg_coefficients(moments, shift):
    def form(a, b):
        anti = {}
        for i, ai in enumerate(a):
            for j, bj in enumerate(b):
                term = bj if ai is None else cmul(ai, bj)
                anti[i + j] = cadd(anti[i + j], term) if i + j in anti else term
        total = None
        for n, coef in anti.items():
            term = cmul(coef, moments[n])
            total = term if total is None else cadd(total, term)
        return total

    one = (jnp.ones_like(shift[0]), jnp.zeros_like(shift[0]))
    x = []
    r = [one]
    p = [one]
    rho = moments[0]
    for iteration in range(ITERS):
        q = [cmul(shift, c) for c in p] + [None]
        for i, c in enumerate(p):
            q[i + 1] = (-c[0], -c[1]) if q[i + 1] is None else csub(q[i + 1], c)
        alpha = cdiv(rho, form(p, q))
        step = [cmul(alpha, c) for c in p]
        x = [cadd(x[i], c) if i < len(x) else c for i, c in enumerate(step)]
        if iteration + 1 < ITERS:
            down = [cmul(alpha, c) for c in q]
            r = [csub(r[i], c) if i < len(r) else (-c[0], -c[1]) for i, c in enumerate(down)]
            rho_new = form(r, r)
            beta = cdiv(rho_new, rho)
            p = [cadd(c, cmul(beta, p[i])) if i < len(p) else c for i, c in enumerate(r)]
            rho = rho_new
    return x


def kernel(
    cells, slabs, poles, v_hbm, pot_hbm, f_ref, corr_ref, en_ref,
    v_ref, pot_ref, e0, e1, e2, pot_halo, diag, stack, payload, from_slab, from_pole,
    fetch, halo_send, halo_recv, slab_send, slab_recv, pole_send, pole_recv,
):
    planes, nx, lanes = pot_ref.shape
    vecs = e0.shape[2]
    nb = vecs // 2
    rows = f_ref.shape[1]
    slab = lax.axis_index("slab")
    pole = lax.axis_index("pole")
    x0 = pole * rows
    up = lax.rem(slab + 1, slabs)
    down = lax.rem(slab + slabs - 1, slabs)
    back = lax.rem(pole + poles - 1, poles)

    parts = fetch.shape[0] - 1
    span = vecs * planes * nx // parts
    fetches = [pltpu.make_async_copy(pot_hbm, pot_ref, fetch.at[parts])]
    for i in range(parts):
        at = pl.ds(i * span, span)
        fetches.append(pltpu.make_async_copy(v_hbm.at[at], v_ref.at[at], fetch.at[i]))
    for copy in fetches:
        copy.start()

    barrier = pltpu.get_barrier_semaphore()
    for d in range(1, slabs):
        pl.semaphore_signal(
            barrier, inc=1, device_id={"slab": lax.rem(slab + d, slabs)}, device_id_type=MESH
        )
    for d in range(1, poles):
        pl.semaphore_signal(
            barrier, inc=1, device_id={"pole": lax.rem(pole + d, poles)}, device_id_type=MESH
        )

    def window(q):
        return lax.rem(x0 + (q - 2 + nx), nx)

    def gather(z):
        for q in range(rows + 4):
            e0[z + 2, q] = v_ref[pl.ds(z * nx + window(q), vecs, stride=planes * nx), :]

    copies = []

    def send(i, src, dst, axis, target):
        copy = pltpu.make_async_remote_copy(
            src_ref=src, dst_ref=dst, send_sem=halo_send.at[i], recv_sem=halo_recv.at[i],
            device_id={axis: target}, device_id_type=MESH,
        )
        copy.start()
        copies.append(copy)
        return copy

    def send_plane(i, z, there, margin, target):
        at = pl.ds(2 - margin, rows + 2 * margin)
        return send(i, e0.at[z + 2, at], e0.at[there + 2, at], "slab", target)

    for copy in fetches:
        copy.wait()
    gather(0)
    gather(planes - 1)
    pl.semaphore_wait(barrier, slabs - 1 + poles - 1)
    near = [
        send(0, pot_ref.at[planes - 1], pot_halo.at[0], "slab", up),
        send(1, pot_ref.at[0], pot_halo.at[1], "slab", down),
        send_plane(2, planes - 1, -1, 1, up),
        send_plane(3, 0, planes, 1, down),
    ]
    for z in range(1, planes - 1):
        gather(z)
    far = [
        send_plane(4, planes - 2, -2, 0, up),
        send_plane(5, 1, planes + 1, 0, down),
    ]

    def spread(ref, z, p):
        for q in range(1, rows + 3):
            line = ref[z, pl.ds(window(q), 1), :] + (3.0 - BASE)
            diag[p, q] = jnp.broadcast_to(line, (vecs, lanes))

    def roll_y(block, by):
        flat = block.reshape(block.shape[0] * vecs, lanes)
        return pltpu.roll(flat, by, 1).reshape(block.shape)

    def apply(src, z, margin):
        p, lo, hi = z + 2, 2 - margin, rows + 2 + margin
        here = src[p, lo:hi]
        beside = src[p - 1, lo:hi] + src[p + 1, lo:hi]
        beside = beside + src[p, lo - 1:hi - 1] + src[p, lo + 1:hi + 1]
        beside = beside + (roll_y(here, 1) + roll_y(here, lanes - 1))
        return diag[p, lo:hi] * here - 0.5 * beside

    def first_power(z, margin):
        e1[z + 2, 2 - margin:rows + 2 + margin] = apply(e0, z, margin)

    def second_power(z):
        e2[z, :rows] = apply(e1, z, 0)

    for z in range(planes):
        spread(pot_ref, z, z + 2)
    for z in range(1, planes - 1):
        first_power(z, 1)
    for copy in near:
        copy.wait_recv()
    first_power(0, 1)
    first_power(planes - 1, 1)
    spread(pot_halo, 0, 1)
    spread(pot_halo, 1, planes + 2)
    for z in range(1, planes - 1):
        second_power(z)
    for copy in far:
        copy.wait_recv()
    first_power(-1, 0)
    first_power(planes, 0)
    second_power(0)
    edge = [send(6, e2.at[0, pl.ds(0, rows)], e2.at[planes, pl.ds(0, rows)], "slab", down)]
    second_power(planes - 1)
    edge.append(send(7, e2.at[pl.ds(0, planes), 0], e2.at[pl.ds(0, planes), rows], "pole", back))

    lo, hi = 2, rows + 2
    sums = [None] * 12

    def split(k, z, u):
        high = u.astype(jnp.bfloat16)
        low = (u - high.astype(jnp.float32)).astype(jnp.bfloat16)
        for r in range(rows):
            at = pl.ds((z * rows + r) * lanes, lanes)
            stack[pl.ds(k * vecs, vecs), at] = high[r]
            stack[pl.ds((4 + k) * vecs, vecs), at] = low[r]

    def collect(n, a, b):
        re = a[:, :nb] * b[:, :nb] - a[:, nb:] * b[:, nb:]
        im = a[:, :nb] * b[:, nb:] + a[:, nb:] * b[:, :nb]
        for i, value in ((n, jnp.sum(re, axis=0)), (6 + n, jnp.sum(im, axis=0))):
            sums[i] = value if sums[i] is None else sums[i] + value

    for z in range(planes):
        u0, u1, u2 = e0[z + 2, lo:hi], e1[z + 2, lo:hi], e2[z, :rows]
        for k, u in enumerate((u0, u1, u2)):
            split(k, z, u)
        for n, (a, b) in enumerate(((u0, u0), (u0, u1), (u1, u1), (u1, u2), (u2, u2))):
            collect(n, a, b)
    for copy in edge:
        copy.wait_recv()
    for z in range(planes):
        u2 = e2[z, :rows]
        ahead = e2[z + 1, :rows] + e2[z, 1:rows + 1] + roll_y(u2, lanes - 1)
        y = 0.5 * (diag[z + 2, lo:hi] * u2 - ahead)
        split(3, z, y)
        collect(5, u2, y)

    full = lax.dot_general(
        stack[...], stack[...], (((1,), (1,)), ((), ())), preferred_element_type=jnp.float32
    )
    half = 4 * vecs
    s = full[:half, :half] + (full[:half, half:] + full[half:, :half] + full[half:, half:])

    lane = lax.broadcasted_iota(jnp.int32, (nb, lanes), 1)
    row = lax.broadcasted_iota(jnp.int32, (nb, lanes), 0)
    first = lax.rem(lane, vecs) < nb

    def hermitian(k):
        re, im = s[k * vecs:k * vecs + nb], s[k * vecs + nb:(k + 1) * vecs]
        return jnp.where(
            first, re + pltpu.roll(im, lanes - nb, 1), re - pltpu.roll(im, nb, 1)
        )

    last = hermitian(2) + jnp.where(lane >= 3 * vecs, pltpu.roll(hermitian(3), vecs, 1), 0.0)
    outer = jnp.where(lane < 2 * vecs, hermitian(0), last)
    middle = hermitian(1)
    for n in range(12):
        value = jnp.sum(sums[n], axis=1, keepdims=True)
        middle = jnp.where(lane == n, value * (2.0 if n in (5, 11) else 1.0), middle)
    payload[0, :nb] = outer
    payload[0, nb:] = middle

    def exchange(source, landing, axis, count, me, send_sem, recv_sem):
        sent = []
        for d in range(1, count):
            copy = pltpu.make_async_remote_copy(
                src_ref=source, dst_ref=landing.at[me], send_sem=send_sem.at[d],
                recv_sem=recv_sem.at[d], device_id={axis: lax.rem(me + d, count)},
                device_id_type=MESH,
            )
            copy.start()
            sent.append(copy)
        landing[me] = source[...]
        for copy in sent:
            copy.wait_recv()
        total = landing[0]
        for i in range(1, count):
            total = total + landing[i]
        return total, sent

    total, sent = exchange(payload.at[0], from_slab, "slab", slabs, slab, slab_send, slab_recv)
    copies += sent
    payload[1] = total
    total, sent = exchange(payload.at[1], from_pole, "pole", poles, pole, pole_send, pole_recv)
    copies += sent
    outer, middle = total[:nb], total[nb:]

    def column(n):
        return jnp.broadcast_to(middle[:, n:n + 1], (nb, lanes))

    moments = [(column(n), column(6 + n)) for n in range(6)]
    shift_re = jnp.zeros((nb, lanes), jnp.float32)
    shift_im, weight_re, weight_im = shift_re, shift_re, shift_re
    for j in range(poles):
        theta = 2.0 * math.pi / poles * (j + 0.5)
        c, t = math.cos(theta), math.sin(theta)
        here = lane >= 0 if j == 0 else lane == j
        shift_re = jnp.where(here, CENTER - BASE + RADIUS * c, shift_re)
        shift_im = jnp.where(here, RADIUS * t, shift_im)
        weight_re = jnp.where(lane == j, RADIUS * c / poles, weight_re)
        weight_im = jnp.where(lane == j, RADIUS * t / poles, weight_im)
    coefs = []
    for x in cocg_coefficients(moments, (shift_re, shift_im)):
        x = cmul((weight_re, weight_im), x)
        coefs.append(tuple(jnp.broadcast_to(jnp.sum(c, axis=1, keepdims=True), (nb, lanes)) for c in x))

    for z in range(planes):
        p = z + 2
        re = im = None
        for (cr, ci), u in zip(coefs, (e0[p, lo:hi], e1[p, lo:hi], e2[z, :rows])):
            ur, ui = u[:, :nb], u[:, nb:]
            tr, ti = cr * ur - ci * ui, cr * ui + ci * ur
            re, im = (tr, ti) if re is None else (re + tr, im + ti)
        f_ref[z, :, :nb] = re
        f_ref[z, :, nb:] = im

    def block(source, n):
        at = n * vecs
        return tuple(
            source if (at + o) % lanes == 0 else pltpu.roll(source, lanes - (at + o), 1)
            for o in (0, nb)
        )

    grams = [
        block(outer, 0), block(outer, 1), block(middle, 1),
        block(middle, 2), block(outer, 2), block(outer, 3),
    ]
    across = [
        tuple(jnp.sum(jnp.where(lane == row, c, 0.0), axis=0, keepdims=True) for c in coef)
        for coef in coefs
    ]

    def quadratic(first_power):
        out = None
        for l in range(3):
            term = None
            for k in range(3):
                t = cmul_conj(coefs[k], grams[k + l + first_power])
                term = t if term is None else cadd(term, t)
            term = cmul(term, across[l])
            out = term if out is None else cadd(out, term)
        return out

    corr = quadratic(0)
    energy = quadratic(1)
    for i in range(2):
        corr_ref[i] = (corr[i] / cells)[:, :nb]
        en_ref[i] = ((energy[i] + BASE * corr[i]) / cells)[:, :nb]
    for copy in copies:
        copy.wait_send()


def on_device(slabs, poles, vectors, potential):
    _, nb, planes, nx, ny = vectors.shape
    rows = nx // poles
    vecs = 2 * nb
    cells = float(planes * slabs * nx * ny)
    flat = vectors.reshape(vecs * planes * nx, ny)
    vmem = pl.BlockSpec(memory_space=pltpu.VMEM)
    whole = pl.BlockSpec(memory_space=pl.ANY)
    field = pltpu.VMEM((planes + 4, rows + 4, vecs, ny), jnp.float32)
    fetches = 4
    dma = pltpu.SemaphoreType.DMA
    filtered, corr, energy = pl.pallas_call(
        functools.partial(kernel, cells, slabs, poles),
        out_shape=(
            jax.ShapeDtypeStruct((planes, rows, vecs, ny), jnp.float32),
            jax.ShapeDtypeStruct((2, nb, nb), jnp.float32),
            jax.ShapeDtypeStruct((2, nb, nb), jnp.float32),
        ),
        in_specs=[whole, whole],
        out_specs=(vmem, vmem, vmem),
        scratch_shapes=[
            pltpu.VMEM(flat.shape, jnp.float32),
            pltpu.VMEM(potential.shape, jnp.float32),
            field,
            field,
            pltpu.VMEM((planes + 1, rows + 1, vecs, ny), jnp.float32),
            pltpu.VMEM((2, nx, ny), jnp.float32),
            field,
            pltpu.VMEM((8 * vecs, planes * rows * ny), jnp.bfloat16),
            pltpu.VMEM((2, vecs, ny), jnp.float32),
            pltpu.VMEM((slabs, vecs, ny), jnp.float32),
            pltpu.VMEM((poles, vecs, ny), jnp.float32),
            dma((fetches + 1,)),
            dma((8,)),
            dma((8,)),
            dma((slabs,)),
            dma((slabs,)),
            dma((poles,)),
            dma((poles,)),
        ],
        compiler_params=pltpu.CompilerParams(
            collective_id=0, has_side_effects=True, vmem_limit_bytes=63 * 1024 * 1024
        ),
    )(flat, potential)
    filtered = filtered.reshape(planes, rows, 2, nb, ny).transpose(2, 3, 0, 1, 4)
    return filtered, corr, energy


def solution(mesh):
    in_specs = (P(None, None, "slab", None, None), P("slab", None, None))
    out_specs = (P(None, None, "slab", "pole", None), P(), P())
    body = functools.partial(on_device, mesh.shape["slab"], mesh.shape["pole"])
    return jax.shard_map(
        body, mesh=mesh, in_specs=in_specs, out_specs=out_specs, check_vma=False
    )
```

profile of v0, /device:TPU:0, one launch (start us, length us, event | category | flops | bytes accessed | tf_op | source)
XLA Modules:
  0.0 32.6 jit_solution(12630477535827636036)
XLA Ops:
  0.6 28.8 %shard_map.49 = (f32[4,4,32,128]{3,2,1,0:T(8,128)}, f32[2,16,16]{2,1,0:T(8,128)}, f32[2,16,16]{2,1,0:T(8,128)}) custom-call(f32[2048,128]{1,0:T(8,128)} %bitcast.5, f32[4,16,128]{2,1,0:T(8,128)} %pot_hbm.1), custom_call_target="tpu_custom_call" | custom-call | tf_op jit(solution)/shard_map/pallas_call | solution.py:352
  29.5 0.0 copy-start.1
  29.5 1.8 %copy.7 = f32[4,4,2,16,128]{4,1,0,3,2:T(4,128)} copy(f32[4,4,2,16,128]{4,3,2,1,0:T(8,128)} %bitcast.7) | data formatting | bytes 524288 | tf_op jit(solution)/shard_map/reshape | solution.py:385
  31.3 0.0 copy-done.1
  31.3 0.0 copy-start
  31.3 0.6 %copy.10 = f32[2,16,16]{2,1,0:T(8,128)} copy(f32[2,16,16]{2,1,0:T(8,128)S(1)} %copy-done.1) | data formatting | bytes 4096
  31.9 0.1 copy-done
  32.0 0.6 %copy.11 = f32[2,16,16]{2,1,0:T(8,128)} copy(f32[2,16,16]{2,1,0:T(8,128)S(1)} %copy-done) | data formatting | bytes 4096
Async XLA Ops:
  29.5 1.8 %copy-start.1 = (f32[2,16,16]{2,1,0:T(8,128)S(1)}, f32[2,16,16]{2,1,0:T(8,128)}, u32[]{:S(2)}) copy-start(f32[2,16,16]{2,1,0:T(8,128)} %get-tuple-element.13) | copy-start | bytes 6148
  31.3 0.7 %copy-start = (f32[2,16,16]{2,1,0:T(8,128)S(1)}, f32[2,16,16]{2,1,0:T(8,128)}, u32[]{:S(2)}) copy-start(f32[2,16,16]{2,1,0:T(8,128)} %get-tuple-element.14) | copy-start | bytes 6148
where the time goes:
time: 32.9 us; the launch traced here: 32.6 us
  Pallas kernels  28.8 us (88%)
  local copies, waits for them, and re-layouts  3.16 us (10%)
  between operations  0.65 us (2%)
    pallas_call x1, Pallas kernels, on_device(): pl.pallas_call(functools.partial(kernel, cells, slabs, poles), out_shape=...  28.8 us
    reshape x1, local copies, waits for them, and re-layouts, on_device(): filtered.reshape(planes, rows, 2, nb, ny).transpose(2, 3, 0, 1, 4)  1.83 us
    unnamed x6, local copies, waits for them, and re-layouts  1.33 us

commit v1 on v0

v1 whole, which is shorter than its diff:
```python
import functools
import math

import jax
import jax.numpy as jnp
from jax import lax
from jax.experimental import pallas as pl
from jax.experimental.pallas import tpu as pltpu
from jax.sharding import PartitionSpec as P

ITERS = 3
CENTER = 2.0
RADIUS = 1.5
BASE = 4.0

MESH = pl.DeviceIdType.MESH


def cmul(a, b):
    return (a[0] * b[0] - a[1] * b[1], a[0] * b[1] + a[1] * b[0])


def cmul_conj(a, b):
    return (a[0] * b[0] + a[1] * b[1], a[0] * b[1] - a[1] * b[0])


def cadd(a, b):
    return (a[0] + b[0], a[1] + b[1])


def csub(a, b):
    return (a[0] - b[0], a[1] - b[1])


def cdiv(n, d):
    inv = 1.0 / (d[0] * d[0] + d[1] * d[1])
    return ((n[0] * d[0] + n[1] * d[1]) * inv, (n[1] * d[0] - n[0] * d[1]) * inv)


def cocg_coefficients(moments, shift):
    def form(a, b):
        anti = {}
        for i, ai in enumerate(a):
            for j, bj in enumerate(b):
                term = bj if ai is None else cmul(ai, bj)
                anti[i + j] = cadd(anti[i + j], term) if i + j in anti else term
        total = None
        for n, coef in anti.items():
            term = cmul(coef, moments[n])
            total = term if total is None else cadd(total, term)
        return total

    one = (jnp.ones_like(shift[0]), jnp.zeros_like(shift[0]))
    x = []
    r = [one]
    p = [one]
    rho = moments[0]
    for iteration in range(ITERS):
        q = [cmul(shift, c) for c in p] + [None]
        for i, c in enumerate(p):
            q[i + 1] = (-c[0], -c[1]) if q[i + 1] is None else csub(q[i + 1], c)
        alpha = cdiv(rho, form(p, q))
        step = [cmul(alpha, c) for c in p]
        x = [cadd(x[i], c) if i < len(x) else c for i, c in enumerate(step)]
        if iteration + 1 < ITERS:
            down = [cmul(alpha, c) for c in q]
            r = [csub(r[i], c) if i < len(r) else (-c[0], -c[1]) for i, c in enumerate(down)]
            rho_new = form(r, r)
            beta = cdiv(rho_new, rho)
            p = [cadd(c, cmul(beta, p[i])) if i < len(p) else c for i, c in enumerate(r)]
            rho = rho_new
    return x


def gather_kernel(
    slabs, poles, v_hbm, pot_hbm, basis_hbm, packed_ref,
    v_ref, pot_ref, e0, e1, e2, pot_halo, diag, stack, last, payload, from_slab, from_pole,
    fetch, store, halo_send, halo_recv, slab_send, slab_recv, pole_send, pole_recv,
):
    planes, nx, lanes = pot_ref.shape
    vecs = e0.shape[2]
    nb = vecs // 2
    rows = basis_hbm.shape[2]
    slab = lax.axis_index("slab")
    pole = lax.axis_index("pole")
    x0 = pole * rows
    up = lax.rem(slab + 1, slabs)
    down = lax.rem(slab + slabs - 1, slabs)
    ahead = lax.rem(pole + 1, poles)
    back = lax.rem(pole + poles - 1, poles)

    order = [0, planes - 1] + list(range(1, planes - 1))
    fetches = {
        z: pltpu.make_async_copy(v_hbm.at[:, z], v_ref.at[z], fetch.at[z]) for z in order
    }
    fetch_pot = pltpu.make_async_copy(pot_hbm, pot_ref, fetch.at[planes])
    for z in order:
        fetches[z].start()
    fetch_pot.start()

    barrier = pltpu.get_barrier_semaphore()
    for d in range(1, slabs):
        pl.semaphore_signal(
            barrier, inc=1, device_id={"slab": lax.rem(slab + d, slabs)}, device_id_type=MESH
        )
    for d in range(1, poles):
        pl.semaphore_signal(
            barrier, inc=1, device_id={"pole": lax.rem(pole + d, poles)}, device_id_type=MESH
        )
    empty = jnp.zeros((vecs, stack.shape[1]), stack.dtype)
    stack[pl.ds(3 * vecs, vecs)] = empty
    stack[pl.ds(7 * vecs, vecs)] = empty

    def window(q):
        return lax.rem(x0 + (q - 2 + nx), nx)

    lines = v_ref.reshape(planes * vecs * nx, lanes)

    def gather(z):
        fetches[z].wait()
        for q in range(rows + 4):
            e0[z + 2, q] = lines[pl.ds(z * vecs * nx + window(q), vecs, stride=nx), :]

    copies = []

    def send(i, src, dst, axis, target):
        copy = pltpu.make_async_remote_copy(
            src_ref=src, dst_ref=dst, send_sem=halo_send.at[i], recv_sem=halo_recv.at[i],
            device_id={axis: target}, device_id_type=MESH,
        )
        copy.start()
        copies.append(copy)
        return copy

    own = pl.ds(2, rows)

    def send_plane(i, z, there, target):
        return send(i, e0.at[z + 2, own], e0.at[there + 2, own], "slab", target)

    gather(0)
    gather(planes - 1)
    fetch_pot.wait()
    pl.semaphore_wait(barrier, slabs - 1 + poles - 1)
    near = [
        send_plane(2, planes - 1, -1, up),
        send_plane(3, 0, planes, down),
        send(0, pot_ref.at[planes - 1], pot_halo.at[0], "slab", up),
        send(1, pot_ref.at[0], pot_halo.at[1], "slab", down),
    ]
    for z in range(1, planes - 1):
        gather(z)
    far = [
        send_plane(4, planes - 2, -2, up),
        send_plane(5, 1, planes + 1, down),
    ]

    def spread(ref, z, p):
        for q in range(1, rows + 3):
            line = ref[z, pl.ds(window(q), 1), :] + (3.0 - BASE)
            diag[p, q] = jnp.broadcast_to(line, (vecs, lanes))

    def roll_y(block, by):
        flat = block.reshape(block.shape[0] * vecs, lanes)
        return pltpu.roll(flat, by, 1).reshape(block.shape)

    def apply(src, z, lo, hi):
        p = z + 2
        here = src[p, lo:hi]
        beside = src[p - 1, lo:hi] + src[p + 1, lo:hi]
        beside = beside + src[p, lo - 1:hi - 1] + src[p, lo + 1:hi + 1]
        beside = beside + (roll_y(here, 1) + roll_y(here, lanes - 1))
        return diag[p, lo:hi] * here - 0.5 * beside

    def first_power(z, lo=2, hi=rows + 2):
        e1[z + 2, lo:hi] = apply(e0, z, lo, hi)

    def second_power(z):
        e2[z, :rows] = apply(e1, z, 2, rows + 2)

    for z in range(planes):
        spread(pot_ref, z, z + 2)
    for z in range(1, planes - 1):
        first_power(z, 1, rows + 3)
    for copy in near:
        copy.wait_recv()
    sides = []
    for i, p in ((6, 1), (8, planes + 2)):
        sides.append(send(i, e0.at[p, 2], e0.at[p, rows + 2], "pole", back))
        sides.append(send(i + 1, e0.at[p, rows + 1], e0.at[p, 1], "pole", ahead))
    first_power(0)
    first_power(planes - 1)
    spread(pot_halo, 0, 1)
    spread(pot_halo, 1, planes + 2)
    for z in range(1, planes - 1):
        second_power(z)
    for copy in sides:
        copy.wait_recv()
    for z in (0, planes - 1):
        first_power(z, 1, 2)
        first_power(z, rows + 2, rows + 3)
    for copy in far:
        copy.wait_recv()
    first_power(-1)
    first_power(planes)
    second_power(0)
    edge = [send(10, e2.at[0, pl.ds(0, rows)], e2.at[planes, pl.ds(0, rows)], "slab", down)]
    second_power(planes - 1)
    edge.append(send(11, e2.at[pl.ds(0, planes), 0], e2.at[pl.ds(0, planes), rows], "pole", back))
    stores = [
        pltpu.make_async_copy(src, basis_hbm.at[k], store.at[k])
        for k, src in enumerate((
            e0.at[pl.ds(2, planes), own],
            e1.at[pl.ds(2, planes), own],
            e2.at[pl.ds(0, planes), pl.ds(0, rows)],
        ))
    ]
    for copy in stores:
        copy.start()

    lo, hi = 2, rows + 2
    sums = [None] * 12

    def split(into, high_row, low_row, z, u):
        high = u.astype(jnp.bfloat16)
        low = (u - high.astype(jnp.float32)).astype(jnp.bfloat16)
        for r in range(rows):
            at = pl.ds((z * rows + r) * lanes, lanes)
            into[pl.ds(high_row, vecs), at] = high[r]
            into[pl.ds(low_row, vecs), at] = low[r]

    def collect(n, a, b):
        re = a[:, :nb] * b[:, :nb] - a[:, nb:] * b[:, nb:]
        im = a[:, :nb] * b[:, nb:] + a[:, nb:] * b[:, :nb]
        for i, value in ((n, jnp.sum(re, axis=0)), (6 + n, jnp.sum(im, axis=0))):
            sums[i] = value if sums[i] is None else sums[i] + value

    def products(a, b):
        full = lax.dot_general(
            a, b, (((1,), (1,)), ((), ())), preferred_element_type=jnp.float32
        )
        h = full.shape[0] // 2
        return full[:h, :h] + (full[:h, h:] + full[h:, :h] + full[h:, h:])

    for z in range(planes):
        u0, u1, u2 = e0[z + 2, lo:hi], e1[z + 2, lo:hi], e2[z, :rows]
        for k, u in enumerate((u0, u1, u2)):
            split(stack, k * vecs, (4 + k) * vecs, z, u)
        for n, (a, b) in enumerate(((u0, u0), (u0, u1), (u1, u1), (u1, u2), (u2, u2))):
            collect(n, a, b)
    s = products(stack[...], stack[...])

    lane = lax.broadcasted_iota(jnp.int32, (nb, lanes), 1)
    row = lax.broadcasted_iota(jnp.int32, (nb, lanes), 0)
    to_left = lanes - nb

    def parts(block):
        re, im = block[:nb], block[nb:]
        return re + pltpu.roll(im, to_left, 1), pltpu.roll(re, to_left, 1) - im

    packed = []
    for k in range(3):
        re, im = parts(s[k * vecs:(k + 1) * vecs])
        packed.append(jnp.where(row <= lax.rem(lane, vecs), re, im))
    pieces = [
        packed[0], pltpu.roll(packed[0], to_left, 1),
        packed[1], pltpu.roll(packed[1], to_left, 1), packed[2],
    ]
    for copy in edge:
        copy.wait_recv()
    for z in range(planes):
        u2 = e2[z, :rows]
        beside = e2[z + 1, :rows] + e2[z, 1:rows + 1] + roll_y(u2, lanes - 1)
        y = 0.5 * (diag[z + 2, lo:hi] * u2 - beside)
        split(last, 0, vecs, z, y)
        collect(5, u2, y)
    second = jnp.concatenate(
        [stack[pl.ds(2 * vecs, vecs)], stack[pl.ds(6 * vecs, vecs)]], axis=0
    )
    m = products(second, last[...])
    m = jnp.concatenate([m, jnp.zeros((vecs, lanes - vecs), jnp.float32)], axis=1)
    re, im = parts(m)
    pieces += [pltpu.roll(re, 5 * nb, 1), pltpu.roll(im, 6 * nb, 1)]
    out = pieces[0]
    for n in range(1, 7):
        out = jnp.where(lane >= n * nb, pieces[n], out)
    for n in range(12):
        value = jnp.sum(sums[n], axis=1, keepdims=True)
        out = jnp.where(lane == 7 * nb + n, value * (2.0 if n in (5, 11) else 1.0), out)
    payload[0] = out

    def exchange(source, landing, axis, count, me, send_sem, recv_sem):
        sent = []
        for d in range(1, count):
            copy = pltpu.make_async_remote_copy(
                src_ref=source, dst_ref=landing.at[me], send_sem=send_sem.at[d],
                recv_sem=recv_sem.at[d], device_id={axis: lax.rem(me + d, count)},
                device_id_type=MESH,
            )
            copy.start()
            sent.append(copy)
        landing[me] = source[...]
        for copy in sent:
            copy.wait_recv()
        total = landing[0]
        for i in range(1, count):
            total = total + landing[i]
        return total, sent

    total, sent = exchange(payload.at[0], from_slab, "slab", slabs, slab, slab_send, slab_recv)
    copies += sent
    payload[1] = total
    total, sent = exchange(payload.at[1], from_pole, "pole", poles, pole, pole_send, pole_recv)
    copies += sent
    packed_ref[...] = total
    for copy in copies:
        copy.wait_send()
    for copy in stores:
        copy.wait()


def filter_kernel(cells, poles, basis_hbm, packed_ref, f_ref, corr_ref, en_ref, basis, fetch):
    _, planes, rows, vecs, lanes = basis.shape
    nb = vecs // 2
    bring = pltpu.make_async_copy(basis_hbm, basis, fetch)
    bring.start()
    packed = packed_ref[...]
    lane = lax.broadcasted_iota(jnp.int32, (nb, lanes), 1)
    row = lax.broadcasted_iota(jnp.int32, (nb, lanes), 0)

    def column(n):
        at = 7 * nb + n
        return jnp.broadcast_to(packed[:, at:at + 1], (nb, lanes))

    moments = [(column(n), column(6 + n)) for n in range(6)]
    shift_re = jnp.zeros((nb, lanes), jnp.float32)
    shift_im, weight_re, weight_im = shift_re, shift_re, shift_re
    for j in range(poles):
        theta = 2.0 * math.pi / poles * (j + 0.5)
        c, t = math.cos(theta), math.sin(theta)
        here = lane >= 0 if j == 0 else lane == j
        shift_re = jnp.where(here, CENTER - BASE + RADIUS * c, shift_re)
        shift_im = jnp.where(here, RADIUS * t, shift_im)
        weight_re = jnp.where(lane == j, RADIUS * c / poles, weight_re)
        weight_im = jnp.where(lane == j, RADIUS * t / poles, weight_im)
    coefs = []
    for x in cocg_coefficients(moments, (shift_re, shift_im)):
        x = cmul((weight_re, weight_im), x)
        coefs.append(
            tuple(jnp.broadcast_to(jnp.sum(c, axis=1, keepdims=True), (nb, lanes)) for c in x)
        )

    bring.wait()
    for z in range(planes):
        re = im = None
        for (cr, ci), u in zip(coefs, (basis[0, z], basis[1, z], basis[2, z])):
            ur, ui = u[:, :nb], u[:, nb:]
            tr, ti = cr * ur - ci * ui, cr * ui + ci * ur
            re, im = (tr, ti) if re is None else (re + tr, im + ti)
        for r in range(rows):
            both = jnp.concatenate([re[r], im[r]], axis=0)
            f_ref[pl.ds(z * rows + r, vecs, stride=planes * rows), :] = both

    square = jnp.concatenate([packed, jnp.zeros((lanes - nb, lanes), jnp.float32)], axis=0)
    turned = jnp.transpose(square)

    def piece(n):
        here = packed if n == 0 else pltpu.roll(packed, lanes - n * nb, 1)
        return here, turned[n * nb:(n + 1) * nb]

    grams = []
    for n in range(5):
        here, across = piece(n)
        re = jnp.where(row <= lane, here, across)
        im = jnp.where(row > lane, here, jnp.where(row < lane, -across, 0.0))
        grams.append((re, im))
    (re, re_t), (im, im_t) = piece(5), piece(6)
    grams.append((re + re_t, im - im_t))
    across = [
        tuple(jnp.sum(jnp.where(lane == row, c, 0.0), axis=0, keepdims=True) for c in coef)
        for coef in coefs
    ]

    def quadratic(first_power):
        out = None
        for l in range(3):
            term = None
            for k in range(3):
                t = cmul_conj(coefs[k], grams[k + l + first_power])
                term = t if term is None else cadd(term, t)
            term = cmul(term, across[l])
            out = term if out is None else cadd(out, term)
        return out

    corr = quadratic(0)
    energy = quadratic(1)
    for i in range(2):
        corr_ref[i] = (corr[i] / cells)[:, :nb]
        en_ref[i] = ((energy[i] + BASE * corr[i]) / cells)[:, :nb]


def on_device(slabs, poles, vectors, potential):
    _, nb, planes, nx, ny = vectors.shape
    rows = nx // poles
    vecs = 2 * nb
    cells = float(planes * slabs * nx * ny)
    vmem = pl.BlockSpec(memory_space=pltpu.VMEM)
    whole = pl.BlockSpec(memory_space=pl.ANY)
    dma = pltpu.SemaphoreType.DMA
    scratch = lambda *shape: pltpu.VMEM(shape, jnp.float32)
    limit = 63 * 1024 * 1024
    basis, packed = pl.pallas_call(
        functools.partial(gather_kernel, slabs, poles),
        out_shape=(
            jax.ShapeDtypeStruct((3, planes, rows, vecs, ny), jnp.float32),
            jax.ShapeDtypeStruct((nb, ny), jnp.float32),
        ),
        in_specs=[whole, whole],
        out_specs=(whole, vmem),
        scratch_shapes=[
            scratch(planes, vecs, nx, ny),
            scratch(planes, nx, ny),
            scratch(planes + 4, rows + 4, vecs, ny),
            scratch(planes + 4, rows + 4, vecs, ny),
            scratch(planes + 1, rows + 1, vecs, ny),
            scratch(2, nx, ny),
            scratch(planes + 4, rows + 4, vecs, ny),
            pltpu.VMEM((8 * vecs, planes * rows * ny), jnp.bfloat16),
            pltpu.VMEM((2 * vecs, planes * rows * ny), jnp.bfloat16),
            scratch(2, nb, ny),
            scratch(slabs, nb, ny),
            scratch(poles, nb, ny),
            dma((planes + 1,)),
            dma((3,)),
            dma((12,)),
            dma((12,)),
            dma((slabs,)),
            dma((slabs,)),
            dma((poles,)),
            dma((poles,)),
        ],
        compiler_params=pltpu.CompilerParams(
            collective_id=0, has_side_effects=True, vmem_limit_bytes=limit
        ),
    )(vectors.reshape(vecs, planes, nx, ny), potential)
    filtered, corr, energy = pl.pallas_call(
        functools.partial(filter_kernel, cells, poles),
        out_shape=(
            jax.ShapeDtypeStruct((vecs * planes * rows, ny), jnp.float32),
            jax.ShapeDtypeStruct((2, nb, nb), jnp.float32),
            jax.ShapeDtypeStruct((2, nb, nb), jnp.float32),
        ),
        in_specs=[whole, vmem],
        out_specs=(vmem, vmem, vmem),
        scratch_shapes=[scratch(3, planes, rows, vecs, ny), dma],
        compiler_params=pltpu.CompilerParams(vmem_limit_bytes=limit),
    )(basis, packed)
    return filtered.reshape(2, nb, planes, rows, ny), corr, energy


def solution(mesh):
    in_specs = (P(None, None, "slab", None, None), P("slab", None, None))
    out_specs = (P(None, None, "slab", "pole", None), P(), P())
    body = functools.partial(on_device, mesh.shape["slab"], mesh.shape["pole"])
    return jax.shard_map(
        body, mesh=mesh, in_specs=in_specs, out_specs=out_specs, check_vma=False
    )
```

time: 32.9 us -> 30.5 us (0.927)
  local copies, waits for them, and re-layouts: 3.16 us -> 0 us
  Pallas kernels: 28.8 us -> 29.6 us
    reshape x1 -> x0, local copies, waits for them, and re-layouts: 1.83 us -> none  [on_device(): filtered.reshape(planes, rows, 2, nb, ny).transpose(2, 3, 0, 1, 4)]
    unnamed x6 -> x0, local copies, waits for them, and re-layouts: 1.33 us -> none
    pallas_call x1 -> x2, Pallas kernels: 28.8 us -> 29.6 us  [the longest x1 26.8 us: on_device(): pl.pallas_call(functools.partial(gather_kernel, slabs, poles), out_shape=...]
where the time goes in v1:
time: 30.5 us; the launch traced here: 30.3 us
  Pallas kernels  29.6 us (97%)
  between operations  0.64 us (2%)
    pallas_call x1, Pallas kernels, on_device(): pl.pallas_call(functools.partial(gather_kernel, slabs, poles), out_shape=...  26.8 us
    pallas_call x1, Pallas kernels, on_device(): pl.pallas_call(functools.partial(filter_kernel, cells, poles), out_shape=...  2.84 us

profile of v1, /device:TPU:0, one launch (start us, length us, event | category | flops | bytes accessed | tf_op | source)
XLA Modules:
  0.0 30.3 jit_solution(4669008039785282487)
XLA Ops:
  0.6 26.8 %shard_map.49 = (f32[3,4,4,32,128]{4,3,2,1,0:T(8,128)}, f32[16,128]{1,0:T(8,128)}) custom-call(f32[32,4,16,128]{3,2,1,0:T(8,128)} %bitcast.2, f32[4,16,128]{2,1,0:T(8,128)} %pot_hbm.1), custom_call_target="tpu_custom_call" | custom-call | tf_op jit(solution)/shard_map/pallas_call | solution.py:411
  27.4 2.8 %shard_map.50 = (f32[512,128]{1,0:T(8,128)}, f32[2,16,16]{2,1,0:T(8,128)}, f32[2,16,16]{2,1,0:T(8,128)}) custom-call(f32[3,4,4,32,128]{4,3,2,1,0:T(8,128)} %get-tuple-element.8.basis_hbm, f32[16,128]{1,0:T(8,128)} %get-tuple-element.9.packed_ref), custom_call_target="tpu_custom_call" | custom-call | tf_op jit(solution)/shard_map/pallas_call | solution.py:445

commit v2 on v1

--- a/solution.py
+++ b/solution.py
@@ -86,8 +86,6 @@
     x0 = pole * rows
     up = lax.rem(slab + 1, slabs)
     down = lax.rem(slab + slabs - 1, slabs)
-    ahead = lax.rem(pole + 1, poles)
-    back = lax.rem(pole + poles - 1, poles)
 
     order = [0, planes - 1] + list(range(1, planes - 1))
     fetches = {
@@ -118,7 +116,7 @@
 
     def gather(z):
         fetches[z].wait()
-        for q in range(rows + 4):
+        for q in range(rows + 5):
             e0[z + 2, q] = lines[pl.ds(z * vecs * nx + window(q), vecs, stride=nx), :]
 
     copies = []
@@ -134,28 +132,29 @@
 
     own = pl.ds(2, rows)
 
-    def send_plane(i, z, there, target):
-        return send(i, e0.at[z + 2, own], e0.at[there + 2, own], "slab", target)
+    def send_plane(i, z, there, lo, hi, target):
+        at = pl.ds(lo, hi - lo)
+        return send(i, e0.at[z + 2, at], e0.at[there + 2, at], "slab", target)
 
     gather(0)
     gather(planes - 1)
     fetch_pot.wait()
     pl.semaphore_wait(barrier, slabs - 1 + poles - 1)
     near = [
-        send_plane(2, planes - 1, -1, up),
-        send_plane(3, 0, planes, down),
+        send_plane(2, planes - 1, -1, 1, rows + 4, up),
+        send_plane(3, 0, planes, 0, rows + 4, down),
         send(0, pot_ref.at[planes - 1], pot_halo.at[0], "slab", up),
-        send(1, pot_ref.at[0], pot_halo.at[1], "slab", down),
+        send(1, pot_ref.at[pl.ds(0, 2)], pot_halo.at[pl.ds(1, 2)], "slab", down),
     ]
-    for z in range(1, planes - 1):
+    gather(1)
+    far = [send_plane(4, 1, planes + 1, 1, rows + 3, down)]
+    for z in range(2, planes - 1):
         gather(z)
-    far = [
-        send_plane(4, planes - 2, -2, up),
-        send_plane(5, 1, planes + 1, down),
-    ]
+    far.append(send_plane(5, planes - 2, -2, 2, rows + 3, up))
+    farthest = send_plane(6, 2, planes + 2, 2, rows + 2, down)
 
     def spread(ref, z, p):
-        for q in range(1, rows + 3):
+        for q in range(1, rows + 4):
             line = ref[z, pl.ds(window(q), 1), :] + (3.0 - BASE)
             diag[p, q] = jnp.broadcast_to(line, (vecs, lanes))
 
@@ -174,38 +173,28 @@
     def first_power(z, lo=2, hi=rows + 2):
         e1[z + 2, lo:hi] = apply(e0, z, lo, hi)
 
-    def second_power(z):
-        e2[z, :rows] = apply(e1, z, 2, rows + 2)
+    def second_power(z, lo=2, hi=rows + 3):
+        e2[z, lo - 2:hi - 2] = apply(e1, z, lo, hi)
 
     for z in range(planes):
         spread(pot_ref, z, z + 2)
     for z in range(1, planes - 1):
-        first_power(z, 1, rows + 3)
+        first_power(z, 1, rows + 4)
     for copy in near:
         copy.wait_recv()
-    sides = []
-    for i, p in ((6, 1), (8, planes + 2)):
-        sides.append(send(i, e0.at[p, 2], e0.at[p, rows + 2], "pole", back))
-        sides.append(send(i + 1, e0.at[p, rows + 1], e0.at[p, 1], "pole", ahead))
-    first_power(0)
-    first_power(planes - 1)
+    first_power(0, 1, rows + 4)
+    first_power(planes - 1, 1, rows + 4)
     spread(pot_halo, 0, 1)
     spread(pot_halo, 1, planes + 2)
+    spread(pot_halo, 2, planes + 3)
     for z in range(1, planes - 1):
         second_power(z)
-    for copy in sides:
-        copy.wait_recv()
-    for z in (0, planes - 1):
-        first_power(z, 1, 2)
-        first_power(z, rows + 2, rows + 3)
     for copy in far:
         copy.wait_recv()
-    first_power(-1)
-    first_power(planes)
+    first_power(-1, 2, rows + 3)
+    first_power(planes, 1, rows + 3)
     second_power(0)
-    edge = [send(10, e2.at[0, pl.ds(0, rows)], e2.at[planes, pl.ds(0, rows)], "slab", down)]
     second_power(planes - 1)
-    edge.append(send(11, e2.at[pl.ds(0, planes), 0], e2.at[pl.ds(0, planes), rows], "pole", back))
     stores = [
         pltpu.make_async_copy(src, basis_hbm.at[k], store.at[k])
         for k, src in enumerate((
@@ -265,8 +254,9 @@
         packed[0], pltpu.roll(packed[0], to_left, 1),
         packed[1], pltpu.roll(packed[1], to_left, 1), packed[2],
     ]
-    for copy in edge:
-        copy.wait_recv()
+    farthest.wait_recv()
+    first_power(planes + 1)
+    second_power(planes, 2, rows + 2)
     for z in range(planes):
         u2 = e2[z, :rows]
         beside = e2[z + 1, :rows] + e2[z, 1:rows + 1] + roll_y(u2, lanes - 1)
@@ -419,11 +409,11 @@
         scratch_shapes=[
             scratch(planes, vecs, nx, ny),
             scratch(planes, nx, ny),
-            scratch(planes + 4, rows + 4, vecs, ny),
-            scratch(planes + 4, rows + 4, vecs, ny),
+            scratch(planes + 5, rows + 5, vecs, ny),
+            scratch(planes + 4, rows + 5, vecs, ny),
             scratch(planes + 1, rows + 1, vecs, ny),
-            scratch(2, nx, ny),
-            scratch(planes + 4, rows + 4, vecs, ny),
+            scratch(3, nx, ny),
+            scratch(planes + 4, rows + 5, vecs, ny),
             pltpu.VMEM((8 * vecs, planes * rows * ny), jnp.bfloat16),
             pltpu.VMEM((2 * vecs, planes * rows * ny), jnp.bfloat16),
             scratch(2, nb, ny),
@@ -431,8 +421,8 @@
             scratch(poles, nb, ny),
             dma((planes + 1,)),
             dma((3,)),
-            dma((12,)),
-            dma((12,)),
+            dma((7,)),
+            dma((7,)),
             dma((slabs,)),
             dma((slabs,)),
             dma((poles,)),

time: 30.5 us -> 31 us (1.016)
  Pallas kernels: 29.6 us -> 30.1 us
    pallas_call x1, Pallas kernels: 26.8 us -> 27.3 us  [on_device(): pl.pallas_call(functools.partial(gather_kernel, slabs, poles), out_shape=...]
where the time goes in v2:
time: 31 us; the launch traced here: 30.7 us
  Pallas kernels  30.1 us (97%)
  between operations  0.64 us (2%)
    pallas_call x1, Pallas kernels, on_device(): pl.pallas_call(functools.partial(gather_kernel, slabs, poles), out_shape=...  27.3 us
    pallas_call x1, Pallas kernels, on_device(): pl.pallas_call(functools.partial(filter_kernel, cells, poles), out_shape=...  2.84 us

profile of v2, /device:TPU:0, one launch (start us, length us, event | category | flops | bytes accessed | tf_op | source)
XLA Modules:
  0.0 30.7 jit_solution(13635139839505931936)
XLA Ops:
  0.6 27.3 %shard_map.49 = (f32[3,4,4,32,128]{4,3,2,1,0:T(8,128)}, f32[16,128]{1,0:T(8,128)}) custom-call(f32[32,4,16,128]{3,2,1,0:T(8,128)} %bitcast.2, f32[4,16,128]{2,1,0:T(8,128)} %pot_hbm.1), custom_call_target="tpu_custom_call" | custom-call | tf_op jit(solution)/shard_map/pallas_call | solution.py:401
  27.9 2.8 %shard_map.50 = (f32[512,128]{1,0:T(8,128)}, f32[2,16,16]{2,1,0:T(8,128)}, f32[2,16,16]{2,1,0:T(8,128)}) custom-call(f32[3,4,4,32,128]{4,3,2,1,0:T(8,128)} %get-tuple-element.8.basis_hbm, f32[16,128]{1,0:T(8,128)} %get-tuple-element.9.packed_ref), custom_call_target="tpu_custom_call" | custom-call | tf_op jit(solution)/shard_map/pallas_call | solution.py:435
